TPU v7x, 128 devices: a whole 4x4x4 slice. The times are simulated.
128 devices in a mesh: grp: 8 (over y, z_hi), lm: 16 (over x, z_lo, core).
Axes of the slice: x: 4, y: 4, z: 4 (z_hi: 2, z_lo: 2; z = z_hi * 2 + z_lo), core: 2. Of those that a mesh axis runs over, the one named last changes fastest.
Arguments:
- embeddings: bfloat16 [32768, 512], P(('grp', 'lm')), may hold values from -14 to 14
- landmarks: bfloat16 [32768, 512], P('lm'), may hold values from -14 to 14
- start_vectors: float32 [32768, 128], P(('grp', 'lm')), may hold values from -10 to 10
- row_weight: float32 [32768], P(('grp', 'lm')), may hold values from 0.1 to 9
- spread: float32 [1], replicated, may hold values from 11.313708 to 33.941124
Outputs:
- subspace: float32 [32768, 128], P(('grp', 'lm'))
All inputs are finite; a program needn't handle non-finite values.
Results may differ from a plain program's by a relative error of at most 0.019.
Values may be sent and summed in bfloat16 or wider, within the bound.
No kernel may reach another device: no remote copies, remote signals or barrier semaphores. Data moves between devices by JAX's collectives and lax.ppermute only.
A program may use at most 128 MiB of HBM per device.

v0:
```python
import jax
import jax.numpy as jnp
from jax import lax
from jax.sharding import PartitionSpec as P

ITERS = 2


def unit_rows(values):
    values = values.astype(jnp.float32)
    scale = lax.rsqrt(jnp.sum(values * values, axis=1, keepdims=True) + 1e-06)
    return (values * scale).astype(jnp.bfloat16)


def kernel_values(rows_unit, marks_unit, gamma):
    cosine = jnp.einsum("rd,ld->rl", rows_unit, marks_unit, preferred_element_type=jnp.float32)
    return jnp.exp(gamma * cosine)


def local(embeddings, landmarks, start_vectors, row_weight, spread):
    own_rows = embeddings.shape[0]
    marks = landmarks.shape[0]
    groups = lax.axis_size("grp")
    members = lax.axis_size("lm")
    total_rows = own_rows * groups * members
    group_rows = own_rows * members
    gamma = spread[0]
    rows_unit = unit_rows(embeddings)
    marks_unit = unit_rows(landmarks)
    sums = jnp.zeros((marks,), jnp.float32)
    weights = jnp.zeros((group_rows,), jnp.float32)
    part_rows = lax.all_gather(rows_unit, "lm", axis=0, tiled=True)
    part_weight = lax.all_gather(row_weight.astype(jnp.bfloat16), "lm", axis=0, tiled=True).astype(
        jnp.float32
    )
    values = kernel_values(part_rows, marks_unit, gamma)
    build_tile = values.astype(jnp.bfloat16)
    weights = lax.dynamic_update_slice_in_dim(weights, part_weight, jnp.int32(0), 0)
    sums = sums + jnp.sum(part_weight[:, None] * values, axis=0)
    mean_sum, weight_sum = lax.psum((sums, jnp.sum(weights)), "grp")
    means = mean_sum / weight_sum
    vectors = start_vectors
    weighted_full = row_weight[:, None] * vectors
    totals = lax.psum(jnp.sum(weighted_full, axis=0), ("grp", "lm"))
    group_weighted = lax.all_gather(weighted_full.astype(jnp.bfloat16), "lm", axis=0, tiled=True)
    for step in range(ITERS):
        side = (
            lax.psum(
                jnp.einsum(
                    "rl,rv->lv", build_tile, group_weighted, preferred_element_type=jnp.float32
                ),
                "grp",
            )
            - means[:, None] * totals[None, :]
        )
        side_b = side.astype(jnp.bfloat16)
        shift = jnp.dot(means, side_b.astype(jnp.float32), precision=lax.Precision.HIGHEST)
        image = lax.psum_scatter(
            weights[:, None]
            * (jnp.dot(build_tile, side_b, preferred_element_type=jnp.float32) - shift[None, :]),
            "lm",
            scatter_dimension=0,
            tiled=True,
        )
        square, column = lax.psum(
            (jnp.sum(image * image, axis=0), jnp.sum(row_weight[:, None] * image, axis=0)),
            ("grp", "lm"),
        )
        scale = jnp.sqrt(square / total_rows + 1e-06)
        vectors = image / scale[None, :]
        totals = column / scale
        if step + 1 < ITERS:
            group_weighted = lax.all_gather(
                (row_weight[:, None] * vectors).astype(jnp.bfloat16), "lm", axis=0, tiled=True
            )
    return vectors


def solution(mesh):
    in_specs = (
        P(("grp", "lm"), None),
        P("lm", None),
        P(("grp", "lm"), None),
        P(("grp", "lm")),
        P(),
    )
    out_specs = P(("grp", "lm"), None)
    return jax.shard_map(local, mesh=mesh, in_specs=in_specs, out_specs=out_specs, check_vma=False)
```

profile of v0, /device:TPU:1, one launch (start us, length us, event | category | flops | bytes accessed | tf_op | source)
XLA Modules:
  0.0 612.0 jit_solution(1574066524591326856)
XLA Ops:
  6.5 0.0 all-gather.5.cloned.1.call-start
  6.5 1.1 fusion.8
  7.6 1.8 fusion.9
  9.4 0.0 all-gather.5.cloned.1.call-update
  9.4 0.0 all-gather.7.cloned.1.call-start
  9.5 1.6 multiply_reduce_fusion.4
  11.1 0.0 all-gather.7.cloned.1.call-update
  11.1 0.0 all-reduce.5.cloned.1.call-start
  11.2 2.1 fusion.3
  13.3 0.7 convert_element_type.35
  14.0 21.3 %all-gather = bf16[16,1,256]{2,1,0:T(2,128)(2,1)S(1)} all-gather(bf16[1,1,256]{2,1,0:T(2,128)(2,1)S(1)} %reshape.21), channel_id=1, replica_groups=mesh['grp'=8,'lm'=16] {'lm'}, dimensions={0}, use_global_device_ids=true | all-gather | bytes 8704 | tf_op jit(solution)/shard_map/all_gather | solution.py:33
  36.0 14.6 %all-gather.5.cloned.1.call-done = bf16[4096,512]{1,0:T(8,128)(2,1)} async-done(((bf16[256,512]{1,0:T(8,128)(2,1)}), bf16[4096,512]{1,0:T(8,128)(2,1)}) %all-gather.5.cloned.1.call-update) | async-done | bytes 4194320 | tf_op jit(solution)/shard_map/all_gather | solution.py:32
  50.6 16.2 %multiply_reduce_fusion = (f32[2048]{0:T(1024)S(1)}, bf16[4096,2048]{1,0:T(8,128)(2,1)}) fusion(f32[4096]{0:T(1024)S(1)} %bitcast.20, f32[]{:T(128)} %bitcast.17, bf16[4096,512]{1,0:T(8,128)(2,1)} %all-gather.5.cloned.1.call-done, bf16[2048,512]{1,0:T(8,128)(2,1)} %param.6, f32[2048]{0:T(1024)S(1)} %add_rsqrt_fusion), kind=kOutput, calls=%fused_computation | convolution fusion | flops 8626632704 | bytes 23101444 | tf_op jit(solution)/shard_map/rd,ld->rl/dot_general | solution.py:16
  66.7 18.1 %all-gather.7.cloned.1.call-done = bf16[4096,128]{1,0:T(8,128)(2,1)} async-done(((bf16[256,128]{1,0:T(8,128)(2,1)}), bf16[4096,128]{1,0:T(8,128)(2,1)}) %all-gather.7.cloned.1.call-update) | async-done | bytes 1048592 | tf_op jit(solution)/shard_map/all_gather | solution.py:45
  84.8 11.6 %fusion.11 = f32[2048,128]{1,0:T(8,128)} fusion(bf16[4096,2048]{1,0:T(8,128)(2,1)} %get-tuple-element.12, bf16[4096,128]{1,0:T(8,128)(2,1)} %all-gather.7.cloned.1.call-done), kind=kOutput, calls=%fused_computation.35 | convolution fusion | flops 2147483648 | bytes 18874368 | tf_op jit(solution)/shard_map/rl,rv->lv/dot_general | solution.py:49
  96.4 0.0 all-reduce.5.cloned.1.call-update
  96.5 0.0 reduce-scatter.3.cloned.1.call-start
  96.5 69.1 %psum.59 = f32[128]{0:T(128)S(1)} all-reduce(f32[128]{0:T(128)S(1)} %get-tuple-element.13), channel_id=1, replica_groups=mesh['grp'=8,'lm'=16] {'grp','lm'}, use_global_device_ids=true, to_apply=%region_8.0 | all-reduce | flops 128 | bytes 1024 | tf_op jit(solution)/shard_map/psum | solution.py:44
  165.7 0.6 convert_reduce_fusion
  166.3 19.9 %all-reduce.1 = (f32[2048]{0:T(1024)S(1)}, f32[]{:T(128)}) all-reduce(f32[2048]{0:T(1024)S(1)} %get-tuple-element.11, f32[]{:T(128)} %convert_reduce_fusion), channel_id=1, replica_groups=mesh['grp'=8,'lm'=16] {'grp'}, use_global_device_ids=true, to_apply=%region_4.0 | all-reduce | flops 2049 | bytes 16392 | tf_op jit(solution)/shard_map/psum | solution.py:40
  186.2 0.6 broadcast_divide_fusion.1
  186.8 0.0 all-reduce.5.cloned.1.call-done
  186.9 1.8 convolution_bitcast_fusion.1
  188.7 0.0 copy-start
  188.7 12.0 %fusion.2 = f32[4096,128]{1,0:T(8,128)} fusion(bf16[4096,2048]{1,0:T(8,128)(2,1)} %get-tuple-element.12, f32[128]{0:T(128)S(1)} %convolution_bitcast_fusion.1, f32[4096]{0:T(1024)S(1)} %bitcast.21, f32[2048,128]{1,0:T(8,128)} %all-reduce.5.cloned.1.call-done, f32[128]{0:T(128)S(1)} %psum.59, f32[2048]{0:T(1024)S(1)} %broadcast_divide_fusion.1), kind=kOutput, calls=%fused_computation.8 | convolution fusion | flops 2149318656 | bytes 19948544 | tf_op jit(solution)/shard_map/dot_general | solution.py:60
  200.7 0.0 reduce-scatter.3.cloned.1.call-update
  200.7 0.0 all-gather.9.cloned.1.call-start
  200.7 61.7 %reduce-scatter.3.cloned.1.call-done = f32[256,128]{1,0:T(8,128)} async-done(((f32[4096,128]{1,0:T(8,128)}), f32[256,128]{1,0:T(8,128)}) %reduce-scatter.3.cloned.1.call-update) | async-done | bytes 131088 | tf_op jit(solution)/shard_map/reduce_scatter | solution.py:58
  262.4 0.0 copy-done
  262.4 1.0 multiply_reduce_fusion.2
  263.5 67.6 %all-reduce = (f32[128]{0:T(128)S(1)}, f32[128]{0:T(128)S(1)}) all-reduce(f32[128]{0:T(128)S(1)} %get-tuple-element.6, f32[128]{0:T(128)S(1)} %get-tuple-element.5), channel_id=1, replica_groups=mesh['grp'=8,'lm'=16] {'grp','lm'}, use_global_device_ids=true, to_apply=%region_11.0 | all-reduce | flops 256 | bytes 2048 | tf_op jit(solution)/shard_map/psum | solution.py:65
  331.1 1.6 multiply_convert_fusion
  332.8 0.0 all-gather.9.cloned.1.call-update
  332.8 0.3 all-reduce.7.cloned.1.call-start
  333.1 29.2 %all-gather.9.cloned.1.call-done = bf16[4096,128]{1,0:T(8,128)(2,1)} async-done(((bf16[256,128]{1,0:T(8,128)(2,1)}), bf16[4096,128]{1,0:T(8,128)(2,1)}) %all-gather.9.cloned.1.call-update) | async-done | bytes 1048592 | tf_op jit(solution)/shard_map/all_gather | solution.py:73
  362.2 11.6 %fusion.12 = f32[2048,128]{1,0:T(8,128)} fusion(bf16[4096,2048]{1,0:T(8,128)(2,1)} %get-tuple-element.12, bf16[4096,128]{1,0:T(8,128)(2,1)} %all-gather.9.cloned.1.call-done), kind=kOutput, calls=%fused_computation.36 | convolution fusion | flops 2147483648 | bytes 18874368 | tf_op jit(solution)/shard_map/rl,rv->lv/dot_general | solution.py:49
  373.9 0.0 all-reduce.7.cloned.1.call-update
  373.9 0.0 reduce-scatter.5.cloned.1.call-start
  373.9 83.7 %all-reduce.7.cloned.1.call-done = f32[2048,128]{1,0:T(8,128)} async-done(((f32[2048,128]{1,0:T(8,128)}), f32[2048,128]{1,0:T(8,128)}) %all-reduce.7.cloned.1.call-update) | async-done | bytes 1048592 | tf_op jit(solution)/shard_map/psum | solution.py:48
  457.6 1.8 convolution_bitcast_fusion
  459.4 12.0 %fusion.1 = f32[4096,128]{1,0:T(8,128)} fusion(bf16[4096,2048]{1,0:T(8,128)(2,1)} %get-tuple-element.12, f32[128]{0:T(128)S(1)} %convolution_bitcast_fusion, f32[4096]{0:T(1024)S(1)} %bitcast.22, f32[2048,128]{1,0:T(8,128)} %all-reduce.7.cloned.1.call-done, f32[128]{0:T(128)S(1)} %get-tuple-element.15, f32[2048]{0:T(1024)S(1)} %broadcast_divide_fusion.1), kind=kOutput, calls=%fused_computation.6 | convolution fusion | flops 2149318656 | bytes 19948544 | tf_op jit(solution)/shard_map/dot_general | solution.py:60
  471.4 0.0 reduce-scatter.5.cloned.1.call-update
  471.4 63.1 %reduce-scatter.5.cloned.1.call-done = f32[256,128]{1,0:T(8,128)} async-done(((f32[4096,128]{1,0:T(8,128)}), f32[256,128]{1,0:T(8,128)}) %reduce-scatter.5.cloned.1.call-update) | async-done | bytes 131088 | tf_op jit(solution)/shard_map/reduce_scatter | solution.py:58
  534.5 1.0 multiply_reduce_fusion.1
  535.4 68.2 %psum.63 = f32[128]{0:T(128)S(1)} all-reduce(f32[128]{0:T(128)S(1)} %multiply_reduce_fusion.1), channel_id=1, replica_groups=mesh['grp'=8,'lm'=16] {'grp','lm'}, use_global_device_ids=true, to_apply=%region_17.0 | all-reduce | flops 128 | bytes 1024 | tf_op jit(solution)/shard_map/psum | solution.py:65
  603.6 1.6 broadcast_divide_fusion
  (6 shorter events, 0.1 us)
Async XLA Ops:
  6.5 44.0 %all-gather.5.cloned.1.call-start = ((), (), s32[]{:S(2)}) async-start(), calls=%async_computation.2 | async-start | bytes 4456448 | tf_op jit(solution)/shard_map/all_gather | solution.py:32
  9.4 75.4 %all-gather.7.cloned.1.call-start = ((), (), s32[]{:S(2)}) async-start(), calls=%async_computation.3 | async-start | bytes 1114112 | tf_op jit(solution)/shard_map/all_gather | solution.py:45
  11.1 175.7 %all-reduce.5.cloned.1.call-start = ((), (), s32[]{:S(2)}) async-start(), calls=%async_computation.4 | async-start | bytes 2097152 | tf_op jit(solution)/shard_map/psum | solution.py:48
  96.5 166.0 %reduce-scatter.3.cloned.1.call-start = ((), (), s32[]{:S(2)}) async-start(), calls=%async_computation.5 | async-start | bytes 2228224 | tf_op jit(solution)/shard_map/reduce_scatter | solution.py:58
  188.7 73.8 %copy-start = (f32[256]{0:T(256)S(1)}, f32[256]{0:T(256)}, u32[]{:S(2)}) copy-start(f32[256]{0:T(256)} %param.8) | copy-start | bytes 3076
  200.7 161.5 %all-gather.9.cloned.1.call-start = ((), (), s32[]{:S(2)}) async-start(), calls=%async_computation.6 | async-start | bytes 1114112 | tf_op jit(solution)/shard_map/all_gather | solution.py:73
  332.8 124.8 %all-reduce.7.cloned.1.call-start = ((), (), s32[]{:S(2)}) async-start(), calls=%async_computation.7 | async-start | bytes 2097152 | tf_op jit(solution)/shard_map/psum | solution.py:48
  373.9 160.6 %reduce-scatter.5.cloned.1.call-start = ((), (), s32[]{:S(2)}) async-start(), calls=%async_computation.8 | async-start | bytes 2228224 | tf_op jit(solution)/shard_map/reduce_scatter | solution.py:58
Sparse Core Ops, SparseCore 0:
  9.5 40.9 all-gather.4
  52.3 32.5 all-gather.6
  96.6 84.5 all-reduce.4
  200.8 61.5 reduce-scatter.2
  332.9 29.2 all-gather.8
  374.0 83.5 all-reduce.6
  471.5 62.8 reduce-scatter.4
where the time goes:
time: 613 us; the launch traced here: 612 us
  waiting for transfers between devices  270 us (44%)
  blocking collectives  246 us (40%)
  matrix products  67 us (11%)
  between operations  14.2 us (2%)
  other arithmetic  13.8 us (2%)
    psum x2, blocking collectives, local(): lax.psum((jnp.sum(image * image, axis=0), jnp.sum(row_weight[:, None] * i...  136 us
    reduce_scatter x2, waiting for transfers between devices, local(): lax.psum_scatter(weights[:, None] * (jnp.dot(build_tile, side_b, preferre...  125 us
    psum x2, waiting for transfers between devices, local(): lax.psum(jnp.einsum('rl,rv->lv', build_tile, group_weighted, preferred_el...  83.7 us
    psum x1, blocking collectives, local(): totals = lax.psum(jnp.sum(weighted_full, axis=0), ('grp', 'lm'))  69.1 us
    all_gather x1, waiting for transfers between devices, local(): lax.all_gather((row_weight[:, None] * vectors).astype(jnp.bfloat16), 'lm'...  29.2 us
    dot_general x2, matrix products, local(): jnp.dot(build_tile, side_b, preferred_element_type=jnp.float32)  24 us
    dot_general x2, matrix products, local(): jnp.einsum('rl,rv->lv', build_tile, group_weighted, preferred_element_typ...  23.2 us
    all_gather x1, blocking collectives, local(): lax.all_gather(row_weight.astype(jnp.bfloat16), 'lm', axis=0, tiled=True)  21.3 us
  transfers between devices with their start and end apart: 7, of which 6 were waited for; matrix products, arithmetic and copies ran while one was open for 4% of the time, Pallas kernels for 0%

commit v1 on v0

--- a/solution.py
+++ b/solution.py
@@ -63,8 +63,11 @@
             tiled=True,
         )
         square, column = lax.psum(
-            (jnp.sum(image * image, axis=0), jnp.sum(row_weight[:, None] * image, axis=0)),
-            ("grp", "lm"),
+            lax.psum(
+                (jnp.sum(image * image, axis=0), jnp.sum(row_weight[:, None] * image, axis=0)),
+                "grp",
+            ),
+            "lm",
         )
         scale = jnp.sqrt(square / total_rows + 1e-06)
         vectors = image / scale[None, :]

time: 613 us -> 583 us (0.951)
  blocking collectives: 246 us -> 220 us
    psum x2, blocking collectives: 136 us -> 41.2 us  [local(): lax.psum((jnp.sum(image * image, axis=0), jnp.sum(row_weight[:, None] * i...]
    psum x0 -> x2, blocking collectives: none -> 68.5 us  [local(): lax.psum(lax.psum((jnp.sum(image * image, axis=0), jnp.sum(row_weight[:,...]
where the time goes in v1:
time: 583 us; the launch traced here: 582 us
  waiting for transfers between devices  267 us (46%)
  blocking collectives  220 us (38%)
  matrix products  67 us (11%)
  between operations  14.2 us (2%)
  other arithmetic  13.8 us (2%)
    reduce_scatter x2, waiting for transfers between devices, local(): lax.psum_scatter(weights[:, None] * (jnp.dot(build_tile, side_b, preferre...  124 us
    psum x2, waiting for transfers between devices, local(): lax.psum(jnp.einsum('rl,rv->lv', build_tile, group_weighted, preferred_el...  83.4 us
    psum x1, blocking collectives, local(): totals = lax.psum(jnp.sum(weighted_full, axis=0), ('grp', 'lm'))  69.1 us
    psum x2, blocking collectives, local(): lax.psum(lax.psum((jnp.sum(image * image, axis=0), jnp.sum(row_weight[:,...  68.5 us
    psum x2, blocking collectives, local(): lax.psum((jnp.sum(image * image, axis=0), jnp.sum(row_weight[:, None] * i...  41.2 us
    all_gather x1, waiting for transfers between devices, local(): lax.all_gather((row_weight[:, None] * vectors).astype(jnp.bfloat16), 'lm'...  26.3 us
    dot_general x2, matrix products, local(): jnp.dot(build_tile, side_b, preferred_element_type=jnp.float32)  24 us
    dot_general x2, matrix products, local(): jnp.einsum('rl,rv->lv', build_tile, group_weighted, preferred_element_typ...  23.2 us
  transfers between devices with their start and end apart: 7, of which 6 were waited for; matrix products, arithmetic and copies ran while one was open for 4% of the time, Pallas kernels for 0%

profile of v1, /device:TPU:1, one launch (start us, length us, event | category | flops | bytes accessed | tf_op | source)
XLA Modules:
  0.0 582.2 jit_solution(3792912268493922208)
XLA Ops:
  6.5 0.0 all-gather.5.cloned.1.call-start
  6.5 1.1 fusion.8
  7.6 1.8 fusion.9
  9.4 0.0 all-gather.5.cloned.1.call-update
  9.4 0.0 all-gather.7.cloned.1.call-start
  9.5 1.6 multiply_reduce_fusion.4
  11.1 0.0 all-gather.7.cloned.1.call-update
  11.1 0.0 all-reduce.6.cloned.1.call-start
  11.2 2.1 fusion.3
  13.3 0.7 convert_element_type.35
  14.0 21.3 %all-gather = bf16[16,1,256]{2,1,0:T(2,128)(2,1)S(1)} all-gather(bf16[1,1,256]{2,1,0:T(2,128)(2,1)S(1)} %reshape.21), channel_id=1, replica_groups=mesh['grp'=8,'lm'=16] {'lm'}, dimensions={0}, use_global_device_ids=true | all-gather | bytes 8704 | tf_op jit(solution)/shard_map/all_gather | solution.py:33
  36.0 14.6 %all-gather.5.cloned.1.call-done = bf16[4096,512]{1,0:T(8,128)(2,1)} async-done(((bf16[256,512]{1,0:T(8,128)(2,1)}), bf16[4096,512]{1,0:T(8,128)(2,1)}) %all-gather.5.cloned.1.call-update) | async-done | bytes 4194320 | tf_op jit(solution)/shard_map/all_gather | solution.py:32
  50.6 16.2 %multiply_reduce_fusion = (f32[2048]{0:T(1024)S(1)}, bf16[4096,2048]{1,0:T(8,128)(2,1)}) fusion(f32[4096]{0:T(1024)S(1)} %bitcast.20, f32[]{:T(128)} %bitcast.17, bf16[4096,512]{1,0:T(8,128)(2,1)} %all-gather.5.cloned.1.call-done, bf16[2048,512]{1,0:T(8,128)(2,1)} %param.6, f32[2048]{0:T(1024)S(1)} %add_rsqrt_fusion), kind=kOutput, calls=%fused_computation | convolution fusion | flops 8626632704 | bytes 23101444 | tf_op jit(solution)/shard_map/rd,ld->rl/dot_general | solution.py:16
  66.7 18.1 %all-gather.7.cloned.1.call-done = bf16[4096,128]{1,0:T(8,128)(2,1)} async-done(((bf16[256,128]{1,0:T(8,128)(2,1)}), bf16[4096,128]{1,0:T(8,128)(2,1)}) %all-gather.7.cloned.1.call-update) | async-done | bytes 1048592 | tf_op jit(solution)/shard_map/all_gather | solution.py:45
  84.8 11.6 %fusion.11 = f32[2048,128]{1,0:T(8,128)} fusion(bf16[4096,2048]{1,0:T(8,128)(2,1)} %get-tuple-element.14, bf16[4096,128]{1,0:T(8,128)(2,1)} %all-gather.7.cloned.1.call-done), kind=kOutput, calls=%fused_computation.35 | convolution fusion | flops 2147483648 | bytes 18874368 | tf_op jit(solution)/shard_map/rl,rv->lv/dot_general | solution.py:49
  96.4 0.0 all-reduce.6.cloned.1.call-update
  96.5 0.0 reduce-scatter.3.cloned.1.call-start
  96.5 69.1 %psum.80 = f32[128]{0:T(128)S(1)} all-reduce(f32[128]{0:T(128)S(1)} %get-tuple-element.15), channel_id=1, replica_groups=mesh['grp'=8,'lm'=16] {'grp','lm'}, use_global_device_ids=true, to_apply=%region_8.0 | all-reduce | flops 128 | bytes 1024 | tf_op jit(solution)/shard_map/psum | solution.py:44
  165.7 0.6 convert_reduce_fusion
  166.3 19.9 %all-reduce.2 = (f32[2048]{0:T(1024)S(1)}, f32[]{:T(128)}) all-reduce(f32[2048]{0:T(1024)S(1)} %get-tuple-element.13, f32[]{:T(128)} %convert_reduce_fusion), channel_id=1, replica_groups=mesh['grp'=8,'lm'=16] {'grp'}, use_global_device_ids=true, to_apply=%region_4.0 | all-reduce | flops 2049 | bytes 16392 | tf_op jit(solution)/shard_map/psum | solution.py:40
  186.2 0.6 broadcast_divide_fusion.1
  186.8 0.0 all-reduce.6.cloned.1.call-done
  186.9 1.8 convolution_bitcast_fusion.1
  188.7 0.0 copy-start
  188.7 12.0 %fusion.2 = f32[4096,128]{1,0:T(8,128)} fusion(bf16[4096,2048]{1,0:T(8,128)(2,1)} %get-tuple-element.14, f32[128]{0:T(128)S(1)} %convolution_bitcast_fusion.1, f32[4096]{0:T(1024)S(1)} %bitcast.21, f32[2048,128]{1,0:T(8,128)} %all-reduce.6.cloned.1.call-done, f32[128]{0:T(128)S(1)} %psum.80, f32[2048]{0:T(1024)S(1)} %broadcast_divide_fusion.1), kind=kOutput, calls=%fused_computation.8 | convolution fusion | flops 2149318656 | bytes 19948544 | tf_op jit(solution)/shard_map/dot_general | solution.py:60
  200.7 0.0 reduce-scatter.3.cloned.1.call-update
  200.7 0.0 all-gather.9.cloned.1.call-start
  200.7 61.1 %reduce-scatter.3.cloned.1.call-done = f32[256,128]{1,0:T(8,128)} async-done(((f32[4096,128]{1,0:T(8,128)}), f32[256,128]{1,0:T(8,128)}) %reduce-scatter.3.cloned.1.call-update) | async-done | bytes 131088 | tf_op jit(solution)/shard_map/reduce_scatter | solution.py:58
  261.9 0.0 copy-done
  261.9 1.0 multiply_reduce_fusion.2
  262.9 20.7 %all-reduce.1 = (f32[128]{0:T(128)S(1)}, f32[128]{0:T(128)S(1)}) all-reduce(f32[128]{0:T(128)S(1)} %get-tuple-element.6, f32[128]{0:T(128)S(1)} %get-tuple-element.5), channel_id=1, replica_groups=mesh['grp'=8,'lm'=16] {'grp'}, use_global_device_ids=true, to_apply=%region_11.0 | all-reduce | flops 256 | bytes 2048 | tf_op jit(solution)/shard_map/psum | solution.py:66
  283.6 34.4 %all-reduce = (f32[128]{0:T(128)S(1)}, f32[128]{0:T(128)S(1)}) all-reduce(f32[128]{0:T(128)S(1)} %get-tuple-element.9, f32[128]{0:T(128)S(1)} %get-tuple-element.10), channel_id=1, replica_groups=mesh['grp'=8,'lm'=16] {'lm'}, use_global_device_ids=true, to_apply=%region_12.0 | all-reduce | flops 256 | bytes 2048 | tf_op jit(solution)/shard_map/psum | solution.py:65
  318.0 1.6 multiply_convert_fusion
  319.6 0.0 all-gather.9.cloned.1.call-update
  319.7 0.0 all-reduce.8.cloned.1.call-start
  319.7 26.3 %all-gather.9.cloned.1.call-done = bf16[4096,128]{1,0:T(8,128)(2,1)} async-done(((bf16[256,128]{1,0:T(8,128)(2,1)}), bf16[4096,128]{1,0:T(8,128)(2,1)}) %all-gather.9.cloned.1.call-update) | async-done | bytes 1048592 | tf_op jit(solution)/shard_map/all_gather | solution.py:76
  346.0 11.6 %fusion.12 = f32[2048,128]{1,0:T(8,128)} fusion(bf16[4096,2048]{1,0:T(8,128)(2,1)} %get-tuple-element.14, bf16[4096,128]{1,0:T(8,128)(2,1)} %all-gather.9.cloned.1.call-done), kind=kOutput, calls=%fused_computation.36 | convolution fusion | flops 2147483648 | bytes 18874368 | tf_op jit(solution)/shard_map/rl,rv->lv/dot_general | solution.py:49
  357.6 0.0 all-reduce.8.cloned.1.call-update
  357.7 0.3 reduce-scatter.5.cloned.1.call-start
  357.9 83.4 %all-reduce.8.cloned.1.call-done = f32[2048,128]{1,0:T(8,128)} async-done(((f32[2048,128]{1,0:T(8,128)}), f32[2048,128]{1,0:T(8,128)}) %all-reduce.8.cloned.1.call-update) | async-done | bytes 1048592 | tf_op jit(solution)/shard_map/psum | solution.py:48
  441.3 1.8 convolution_bitcast_fusion
  443.1 12.0 %fusion.1 = f32[4096,128]{1,0:T(8,128)} fusion(bf16[4096,2048]{1,0:T(8,128)(2,1)} %get-tuple-element.14, f32[128]{0:T(128)S(1)} %convolution_bitcast_fusion, f32[4096]{0:T(1024)S(1)} %bitcast.22, f32[2048,128]{1,0:T(8,128)} %all-reduce.8.cloned.1.call-done, f32[128]{0:T(128)S(1)} %get-tuple-element.17, f32[2048]{0:T(1024)S(1)} %broadcast_divide_fusion.1), kind=kOutput, calls=%fused_computation.6 | convolution fusion | flops 2149318656 | bytes 19948544 | tf_op jit(solution)/shard_map/dot_general | solution.py:60
  455.1 0.0 reduce-scatter.5.cloned.1.call-update
  455.2 63.0 %reduce-scatter.5.cloned.1.call-done = f32[256,128]{1,0:T(8,128)} async-done(((f32[4096,128]{1,0:T(8,128)}), f32[256,128]{1,0:T(8,128)}) %reduce-scatter.5.cloned.1.call-update) | async-done | bytes 131088 | tf_op jit(solution)/shard_map/reduce_scatter | solution.py:58
  518.2 1.0 multiply_reduce_fusion.1
  519.2 20.6 %psum.86 = f32[128]{0:T(128)S(1)} all-reduce(f32[128]{0:T(128)S(1)} %multiply_reduce_fusion.1), channel_id=1, replica_groups=mesh['grp'=8,'lm'=16] {'grp'}, use_global_device_ids=true, to_apply=%region_19.0 | all-reduce | flops 128 | bytes 1024 | tf_op jit(solution)/shard_map/psum | solution.py:66
  539.7 34.0 %psum.87 = f32[128]{0:T(128)S(1)} all-reduce(f32[128]{0:T(128)S(1)} %psum.86), channel_id=1, replica_groups=mesh['grp'=8,'lm'=16] {'lm'}, use_global_device_ids=true, to_apply=%region_20.0 | all-reduce | flops 128 | bytes 1024 | tf_op jit(solution)/shard_map/psum | solution.py:65
  573.8 1.6 broadcast_divide_fusion
  (6 shorter events, 0.1 us)
Async XLA Ops:
  6.5 44.0 %all-gather.5.cloned.1.call-start = ((), (), s32[]{:S(2)}) async-start(), calls=%async_computation.2 | async-start | bytes 4456448 | tf_op jit(solution)/shard_map/all_gather | solution.py:32
  9.4 75.4 %all-gather.7.cloned.1.call-start = ((), (), s32[]{:S(2)}) async-start(), calls=%async_computation.3 | async-start | bytes 1114112 | tf_op jit(solution)/shard_map/all_gather | solution.py:45
  11.1 175.7 %all-reduce.6.cloned.1.call-start = ((), (), s32[]{:S(2)}) async-start(), calls=%async_computation.4 | async-start | bytes 2097152 | tf_op jit(solution)/shard_map/psum | solution.py:48
  96.5 165.4 %reduce-scatter.3.cloned.1.call-start = ((), (), s32[]{:S(2)}) async-start(), calls=%async_computation.5 | async-start | bytes 2228224 | tf_op jit(solution)/shard_map/reduce_scatter | solution.py:58
  188.7 73.2 %copy-start = (f32[256]{0:T(256)S(1)}, f32[256]{0:T(256)}, u32[]{:S(2)}) copy-start(f32[256]{0:T(256)} %param.8) | copy-start | bytes 3076
  200.7 145.3 %all-gather.9.cloned.1.call-start = ((), (), s32[]{:S(2)}) async-start(), calls=%async_computation.6 | async-start | bytes 1114112 | tf_op jit(solution)/shard_map/all_gather | solution.py:76
  319.7 121.7 %all-reduce.8.cloned.1.call-start = ((), (), s32[]{:S(2)}) async-start(), calls=%async_computation.7 | async-start | bytes 2097152 | tf_op jit(solution)/shard_map/psum | solution.py:48
  357.7 160.6 %reduce-scatter.5.cloned.1.call-start = ((), (), s32[]{:S(2)}) async-start(), calls=%async_computation.8 | async-start | bytes 2228224 | tf_op jit(solution)/shard_map/reduce_scatter | solution.py:58
Sparse Core Ops, SparseCore 0:
  9.5 40.9 all-gather.4
  52.3 32.5 all-gather.6
  96.6 84.5 all-reduce.5
  200.8 60.9 reduce-scatter.2
  319.8 26.1 all-gather.8
  357.8 83.5 all-reduce.7
  455.3 62.8 reduce-scatter.4
